TPU v7x, 32 devices: a whole 2x2x4 slice. The times are simulated.
32 devices in a mesh: row: 8 (over y, x, core), col: 4 (over z).
Axes of the slice: x: 2, y: 2, z: 4, core: 2. Of those that a mesh axis runs over, the one named last changes fastest.
Arguments:
- collocation: bfloat16 [32768, 2048], P('col', 'row'), may hold values from -6 to 6
- greens: bfloat16 [2, 256, 2048], P(None, None, 'row'), may hold values from -0.0078125 to 0.0078125
- trial_orbitals: bfloat16 [256, 2048], P(None, 'row'), may hold values from -0.125 to 0.125
- coulomb: bfloat16 [4, 8192, 32768], P(None, 'row', 'col'), may hold values from -0.03125 to 0.03125
Outputs:
- gradient: bfloat16 [256, 2, 2048], P('col', None, 'row')
All inputs are finite; a program needn't handle non-finite values.
Results may differ from a plain program's by a relative error of at most 0.039.
Values may be sent and summed in bfloat16 or wider, within the bound.
A program may use at most 192 MiB of HBM per device.

v0:
```python
import math

import jax
import jax.numpy as jnp
from jax import lax
from jax.sharding import PartitionSpec as P

P_SIZE = 32768


def make_forces(exchange_sum, potential, orbit_part, walkers, occupied):
    orbit_wide = orbit_part.astype(jnp.float32)
    pieces = []
    for walker in range(walkers):
        pieces.append(
            potential[:, walker : walker + 1] * orbit_wide
            - exchange_sum[:, walker * occupied : (walker + 1) * occupied]
        )
    return jnp.concatenate(pieces, axis=1).astype(jnp.bfloat16)


def on_device(collocation, greens, trial_orbitals, coulomb):
    walkers, occupied, basis_local = greens.shape
    stacked = jnp.concatenate([trial_orbitals[None], greens], axis=0).reshape(
        (walkers + 1) * occupied, basis_local
    )
    partial_value = jnp.einsum(
        "pm,km->pk", collocation, stacked, preferred_element_type=jnp.float32
    )
    own_points = lax.psum_scatter(
        partial_value.astype(jnp.bfloat16), "row", scatter_dimension=0, tiled=True
    )
    col_orbitals = lax.all_gather(own_points[:, :occupied], "row", axis=0, tiled=True)
    kernel_rows = coulomb.reshape(coulomb.shape[0] * coulomb.shape[1], coulomb.shape[2])
    col_count = kernel_rows.shape[1]
    start_totals = (
        jnp.zeros((col_count, walkers * occupied), jnp.float32),
        jnp.zeros((col_count, walkers), jnp.float32),
    )
    shard_rows = lax.all_gather(own_points, "col", axis=0, tiled=True)
    height = shard_rows.shape[0]
    step_rows = math.gcd(height, 512)

    def advance(turn, inner):
        k_total, u_total = inner
        block_rows = lax.dynamic_slice_in_dim(shard_rows, turn * step_rows, step_rows, 0)
        v_rows = lax.dynamic_slice_in_dim(kernel_rows, turn * step_rows, step_rows, 0)
        x_rows = block_rows[:, :occupied]
        k_parts = []
        u_parts = []
        for walker in range(walkers):
            theta_rows = block_rows[:, (walker + 1) * occupied : (walker + 2) * occupied]
            t_tile = jnp.einsum(
                "pi,qi->pq", theta_rows, col_orbitals, preferred_element_type=jnp.float32
            )
            amplitude = (v_rows * t_tile).astype(jnp.bfloat16)
            k_parts.append(
                jnp.einsum("pq,pi->qi", amplitude, x_rows, preferred_element_type=jnp.float32)
            )
            density = jnp.sum(
                x_rows.astype(jnp.float32) * theta_rows.astype(jnp.float32), axis=1
            ).astype(jnp.bfloat16)
            u_parts.append(
                jnp.einsum("p,pq->q", density, v_rows, preferred_element_type=jnp.float32)
            )
        return (k_total + jnp.concatenate(k_parts, axis=1), u_total + jnp.stack(u_parts, axis=1))

    k_total, u_total = lax.fori_loop(0, height // step_rows, advance, start_totals)
    k_whole, u_whole = (
        lax.psum(k_total.astype(jnp.bfloat16), "row").astype(jnp.float32),
        lax.psum(u_total.astype(jnp.bfloat16), "row").astype(jnp.float32),
    )
    forces = make_forces(k_whole, u_whole, col_orbitals, walkers, occupied)
    width_rows = occupied // lax.axis_size("col") * lax.axis_size("col")
    terms = []
    for walker in range(walkers):
        force_cols = lax.dynamic_slice_in_dim(forces, walker * occupied, width_rows, 1)
        terms.append(
            jnp.einsum("qi,qm->im", force_cols, collocation, preferred_element_type=jnp.float32)
        )
    gradient = lax.psum_scatter(
        jnp.stack(terms, axis=1).astype(jnp.bfloat16), "col", scatter_dimension=0, tiled=True
    ).astype(jnp.float32)
    return (gradient * P_SIZE ** (-0.5)).astype(jnp.bfloat16)


def solution(mesh):
    return jax.shard_map(
        on_device,
        mesh=mesh,
        in_specs=(P("col", "row"), P(None, None, "row"), P(None, "row"), P(None, "row", "col")),
        out_specs=P("col", None, "row"),
        check_vma=False,
    )
```

profile of v0, /device:TPU:0, one launch (start us, length us, event | category | flops | bytes accessed | tf_op | source)
XLA Modules:
  0.0 830.1 jit_solution(16708627238823192573)
XLA Ops:
  6.5 1.0 pad_maximum_fusion
  7.6 8.6 %fusion.12 = bf16[8192,768]{0,1:T(8,128)(2,1)} fusion(bf16[768,256]{1,0:T(8,128)(2,1)S(1)} %bitcast.43, bf16[8192,256]{1,0:T(8,128)(2,1)} %param.6), kind=kOutput, calls=%fused_computation.22 | convolution fusion | flops 3227516928 | bytes 17170432 | tf_op jit(solution)/shard_map/pm,km->pk/dot_general | solution.py:27
  16.2 95.2 %reduce-scatter.3.cloned.1.call-done = bf16[1024,768]{0,1:T(8,128)(2,1)} async-done(((bf16[8192,768]{0,1:T(8,128)(2,1)}), bf16[1024,768]{0,1:T(8,128)(2,1)}) %reduce-scatter.3.cloned.1.call-update) | async-done | bytes 1572880 | tf_op jit(solution)/shard_map/reduce_scatter | solution.py:30
  111.4 1.9 slice.44
  114.1 36.1 %all-gather.5.cloned.1.call-done = bf16[8192,256]{0,1:T(8,128)(2,1)} async-done(((bf16[1024,256]{0,1:T(8,128)(2,1)}), bf16[8192,256]{0,1:T(8,128)(2,1)}) %all-gather.5.cloned.1.call-update) | async-done | bytes 4194320 | tf_op jit(solution)/shard_map/all_gather | solution.py:33
  150.2 6.3 copy.6
  156.5 110.6 %all-gather.3.cloned.1.call-done = bf16[4096,768]{0,1:T(8,128)(2,1)} async-done(((bf16[1024,768]{0,1:T(8,128)(2,1)}), bf16[4096,768]{0,1:T(8,128)(2,1)}) %all-gather.3.cloned.1.call-update) | async-done | bytes 6291472 | tf_op jit(solution)/shard_map/all_gather | solution.py:40
  267.1 375.4 %while.16 = (s32[]{:T(128)}, f32[8192,512]{0,1:T(8,128)}, f32[8192,2]{0,1:T(2,128)S(1)}, bf16[4096,8192]{1,0:T(8,128)(2,1)}, bf16[4096,768]{0,1:T(8,128)(2,1)}, ...) while((s32[]{:T(128)}, f32[8192,512]{0,1:T(8,128)}, ...), condition=%wide.region_4.0_spmd.clone, body=%wide.region_1.0_spmd.clone.sunk | while | flops 8645426176 | bytes 114305240 | solution.py:68
  267.2 1.2 constant_dynamic-slice_fusion.8
  269.0 4.6 convolution_bitcast_fusion.5
  273.6 4.6 convolution_bitcast_fusion.4
  278.3 9.7 %fusion.66 = f32[8192,256]{0,1:T(8,128)} fusion(bf16[512,256]{0,1:T(8,128)(2,1)S(1)} %get-tuple-element.206, bf16[8192,256]{1,0:T(8,128)(2,1)} %get-tuple-element.239, bf16[4096,8192]{1,0:T(8,128)(2,1)} %get-tuple-element.237, s32[]{:T(128)S(6)} %select_n.10, bf16[4096,768]{0,1:T(8,128)(2,1)} %get-tuple-element.238), kind=kOutput, calls=%fused_computation.10.clone.1 | convolution fusion | flops 4307550208 | bytes 21496832 | tf_op jit(solution)/shard_map/while/body/eval_jaxpr/pq,pi->qi/dot_general | solution.py:58
  287.9 9.7 %fusion.65 = f32[8192,256]{0,1:T(8,128)} fusion(bf16[512,256]{0,1:T(8,128)(2,1)S(1)} %get-tuple-element.205, bf16[8192,256]{1,0:T(8,128)(2,1)} %get-tuple-element.239, bf16[4096,8192]{1,0:T(8,128)(2,1)} %get-tuple-element.237, s32[]{:T(128)S(6)} %select_n.10, bf16[4096,768]{0,1:T(8,128)(2,1)} %get-tuple-element.238), kind=kOutput, calls=%fused_computation.9.clone.1 | convolution fusion | flops 4307550208 | bytes 21496832 | tf_op jit(solution)/shard_map/while/body/eval_jaxpr/pq,pi->qi/dot_general | solution.py:58
  297.6 13.1 %maximum_add_fusion.4 = f32[8192,512]{0,1:T(8,128)} fusion(f32[8192,256]{0,1:T(8,128)} %fusion.65, f32[8192,256]{0,1:T(8,128)} %fusion.66, f32[8192,512]{0,1:T(8,128)} %get-tuple-element.223, pred[]{:T(512)S(6)} %compare.3), kind=kLoop, calls=%fused_computation.4.clone.1 | loop fusion | flops 12582912 | bytes 50331648 | tf_op jit(solution)/shard_map/while/body/eval_jaxpr/add | solution.py:66
  310.7 1.2 constant_dynamic-slice_fusion.8
  312.5 4.6 convolution_bitcast_fusion.5
  317.1 4.6 convolution_bitcast_fusion.4
  321.8 9.7 %fusion.66 = f32[8192,256]{0,1:T(8,128)} fusion(bf16[512,256]{0,1:T(8,128)(2,1)S(1)} %get-tuple-element.206, bf16[8192,256]{1,0:T(8,128)(2,1)} %get-tuple-element.239, bf16[4096,8192]{1,0:T(8,128)(2,1)} %get-tuple-element.237, s32[]{:T(128)S(6)} %select_n.10, bf16[4096,768]{0,1:T(8,128)(2,1)} %get-tuple-element.238), kind=kOutput, calls=%fused_computation.10.clone.1 | convolution fusion | flops 4307550208 | bytes 21496832 | tf_op jit(solution)/shard_map/while/body/eval_jaxpr/pq,pi->qi/dot_general | solution.py:58
  331.4 9.7 %fusion.65 = f32[8192,256]{0,1:T(8,128)} fusion(bf16[512,256]{0,1:T(8,128)(2,1)S(1)} %get-tuple-element.205, bf16[8192,256]{1,0:T(8,128)(2,1)} %get-tuple-element.239, bf16[4096,8192]{1,0:T(8,128)(2,1)} %get-tuple-element.237, s32[]{:T(128)S(6)} %select_n.10, bf16[4096,768]{0,1:T(8,128)(2,1)} %get-tuple-element.238), kind=kOutput, calls=%fused_computation.9.clone.1 | convolution fusion | flops 4307550208 | bytes 21496832 | tf_op jit(solution)/shard_map/while/body/eval_jaxpr/pq,pi->qi/dot_general | solution.py:58
  341.1 17.0 %maximum_add_fusion.4 = f32[8192,512]{0,1:T(8,128)} fusion(f32[8192,256]{0,1:T(8,128)} %fusion.65, f32[8192,256]{0,1:T(8,128)} %fusion.66, f32[8192,512]{0,1:T(8,128)} %get-tuple-element.223, pred[]{:T(512)S(6)} %compare.3), kind=kLoop, calls=%fused_computation.4.clone.1 | loop fusion | flops 12582912 | bytes 50331648 | tf_op jit(solution)/shard_map/while/body/eval_jaxpr/add | solution.py:66
  358.1 1.2 constant_dynamic-slice_fusion.8
  359.9 4.6 convolution_bitcast_fusion.5
  364.5 4.6 convolution_bitcast_fusion.4
  369.2 9.7 %fusion.66 = f32[8192,256]{0,1:T(8,128)} fusion(bf16[512,256]{0,1:T(8,128)(2,1)S(1)} %get-tuple-element.206, bf16[8192,256]{1,0:T(8,128)(2,1)} %get-tuple-element.239, bf16[4096,8192]{1,0:T(8,128)(2,1)} %get-tuple-element.237, s32[]{:T(128)S(6)} %select_n.10, bf16[4096,768]{0,1:T(8,128)(2,1)} %get-tuple-element.238), kind=kOutput, calls=%fused_computation.10.clone.1 | convolution fusion | flops 4307550208 | bytes 21496832 | tf_op jit(solution)/shard_map/while/body/eval_jaxpr/pq,pi->qi/dot_general | solution.py:58
  378.8 9.7 %fusion.65 = f32[8192,256]{0,1:T(8,128)} fusion(bf16[512,256]{0,1:T(8,128)(2,1)S(1)} %get-tuple-element.205, bf16[8192,256]{1,0:T(8,128)(2,1)} %get-tuple-element.239, bf16[4096,8192]{1,0:T(8,128)(2,1)} %get-tuple-element.237, s32[]{:T(128)S(6)} %select_n.10, bf16[4096,768]{0,1:T(8,128)(2,1)} %get-tuple-element.238), kind=kOutput, calls=%fused_computation.9.clone.1 | convolution fusion | flops 4307550208 | bytes 21496832 | tf_op jit(solution)/shard_map/while/body/eval_jaxpr/pq,pi->qi/dot_general | solution.py:58
  388.5 17.0 %maximum_add_fusion.4 = f32[8192,512]{0,1:T(8,128)} fusion(f32[8192,256]{0,1:T(8,128)} %fusion.65, f32[8192,256]{0,1:T(8,128)} %fusion.66, f32[8192,512]{0,1:T(8,128)} %get-tuple-element.223, pred[]{:T(512)S(6)} %compare.3), kind=kLoop, calls=%fused_computation.4.clone.1 | loop fusion | flops 12582912 | bytes 50331648 | tf_op jit(solution)/shard_map/while/body/eval_jaxpr/add | solution.py:66
  405.5 1.2 constant_dynamic-slice_fusion.8
  407.3 4.6 convolution_bitcast_fusion.5
  411.9 4.6 convolution_bitcast_fusion.4
  416.6 9.7 %fusion.66 = f32[8192,256]{0,1:T(8,128)} fusion(bf16[512,256]{0,1:T(8,128)(2,1)S(1)} %get-tuple-element.206, bf16[8192,256]{1,0:T(8,128)(2,1)} %get-tuple-element.239, bf16[4096,8192]{1,0:T(8,128)(2,1)} %get-tuple-element.237, s32[]{:T(128)S(6)} %select_n.10, bf16[4096,768]{0,1:T(8,128)(2,1)} %get-tuple-element.238), kind=kOutput, calls=%fused_computation.10.clone.1 | convolution fusion | flops 4307550208 | bytes 21496832 | tf_op jit(solution)/shard_map/while/body/eval_jaxpr/pq,pi->qi/dot_general | solution.py:58
  426.3 9.7 %fusion.65 = f32[8192,256]{0,1:T(8,128)} fusion(bf16[512,256]{0,1:T(8,128)(2,1)S(1)} %get-tuple-element.205, bf16[8192,256]{1,0:T(8,128)(2,1)} %get-tuple-element.239, bf16[4096,8192]{1,0:T(8,128)(2,1)} %get-tuple-element.237, s32[]{:T(128)S(6)} %select_n.10, bf16[4096,768]{0,1:T(8,128)(2,1)} %get-tuple-element.238), kind=kOutput, calls=%fused_computation.9.clone.1 | convolution fusion | flops 4307550208 | bytes 21496832 | tf_op jit(solution)/shard_map/while/body/eval_jaxpr/pq,pi->qi/dot_general | solution.py:58
  435.9 17.0 %maximum_add_fusion.4 = f32[8192,512]{0,1:T(8,128)} fusion(f32[8192,256]{0,1:T(8,128)} %fusion.65, f32[8192,256]{0,1:T(8,128)} %fusion.66, f32[8192,512]{0,1:T(8,128)} %get-tuple-element.223, pred[]{:T(512)S(6)} %compare.3), kind=kLoop, calls=%fused_computation.4.clone.1 | loop fusion | flops 12582912 | bytes 50331648 | tf_op jit(solution)/shard_map/while/body/eval_jaxpr/add | solution.py:66
  452.9 1.2 constant_dynamic-slice_fusion.8
  454.8 4.6 convolution_bitcast_fusion.5
  459.3 4.6 convolution_bitcast_fusion.4
  464.0 9.7 %fusion.66 = f32[8192,256]{0,1:T(8,128)} fusion(bf16[512,256]{0,1:T(8,128)(2,1)S(1)} %get-tuple-element.206, bf16[8192,256]{1,0:T(8,128)(2,1)} %get-tuple-element.239, bf16[4096,8192]{1,0:T(8,128)(2,1)} %get-tuple-element.237, s32[]{:T(128)S(6)} %select_n.10, bf16[4096,768]{0,1:T(8,128)(2,1)} %get-tuple-element.238), kind=kOutput, calls=%fused_computation.10.clone.1 | convolution fusion | flops 4307550208 | bytes 21496832 | tf_op jit(solution)/shard_map/while/body/eval_jaxpr/pq,pi->qi/dot_general | solution.py:58
  473.7 9.7 %fusion.65 = f32[8192,256]{0,1:T(8,128)} fusion(bf16[512,256]{0,1:T(8,128)(2,1)S(1)} %get-tuple-element.205, bf16[8192,256]{1,0:T(8,128)(2,1)} %get-tuple-element.239, bf16[4096,8192]{1,0:T(8,128)(2,1)} %get-tuple-element.237, s32[]{:T(128)S(6)} %select_n.10, bf16[4096,768]{0,1:T(8,128)(2,1)} %get-tuple-element.238), kind=kOutput, calls=%fused_computation.9.clone.1 | convolution fusion | flops 4307550208 | bytes 21496832 | tf_op jit(solution)/shard_map/while/body/eval_jaxpr/pq,pi->qi/dot_general | solution.py:58
  483.3 17.0 %maximum_add_fusion.4 = f32[8192,512]{0,1:T(8,128)} fusion(f32[8192,256]{0,1:T(8,128)} %fusion.65, f32[8192,256]{0,1:T(8,128)} %fusion.66, f32[8192,512]{0,1:T(8,128)} %get-tuple-element.223, pred[]{:T(512)S(6)} %compare.3), kind=kLoop, calls=%fused_computation.4.clone.1 | loop fusion | flops 12582912 | bytes 50331648 | tf_op jit(solution)/shard_map/while/body/eval_jaxpr/add | solution.py:66
  500.3 1.2 constant_dynamic-slice_fusion.8
  502.2 4.6 convolution_bitcast_fusion.5
  506.7 4.6 convolution_bitcast_fusion.4
  511.4 9.7 %fusion.66 = f32[8192,256]{0,1:T(8,128)} fusion(bf16[512,256]{0,1:T(8,128)(2,1)S(1)} %get-tuple-element.206, bf16[8192,256]{1,0:T(8,128)(2,1)} %get-tuple-element.239, bf16[4096,8192]{1,0:T(8,128)(2,1)} %get-tuple-element.237, s32[]{:T(128)S(6)} %select_n.10, bf16[4096,768]{0,1:T(8,128)(2,1)} %get-tuple-element.238), kind=kOutput, calls=%fused_computation.10.clone.1 | convolution fusion | flops 4307550208 | bytes 21496832 | tf_op jit(solution)/shard_map/while/body/eval_jaxpr/pq,pi->qi/dot_general | solution.py:58
  521.1 9.7 %fusion.65 = f32[8192,256]{0,1:T(8,128)} fusion(bf16[512,256]{0,1:T(8,128)(2,1)S(1)} %get-tuple-element.205, bf16[8192,256]{1,0:T(8,128)(2,1)} %get-tuple-element.239, bf16[4096,8192]{1,0:T(8,128)(2,1)} %get-tuple-element.237, s32[]{:T(128)S(6)} %select_n.10, bf16[4096,768]{0,1:T(8,128)(2,1)} %get-tuple-element.238), kind=kOutput, calls=%fused_computation.9.clone.1 | convolution fusion | flops 4307550208 | bytes 21496832 | tf_op jit(solution)/shard_map/while/body/eval_jaxpr/pq,pi->qi/dot_general | solution.py:58
  530.8 17.0 %maximum_add_fusion.4 = f32[8192,512]{0,1:T(8,128)} fusion(f32[8192,256]{0,1:T(8,128)} %fusion.65, f32[8192,256]{0,1:T(8,128)} %fusion.66, f32[8192,512]{0,1:T(8,128)} %get-tuple-element.223, pred[]{:T(512)S(6)} %compare.3), kind=kLoop, calls=%fused_computation.4.clone.1 | loop fusion | flops 12582912 | bytes 50331648 | tf_op jit(solution)/shard_map/while/body/eval_jaxpr/add | solution.py:66
  547.8 1.2 constant_dynamic-slice_fusion.8
  549.6 4.6 convolution_bitcast_fusion.5
  554.2 4.6 convolution_bitcast_fusion.4
  558.9 9.7 %fusion.66 = f32[8192,256]{0,1:T(8,128)} fusion(bf16[512,256]{0,1:T(8,128)(2,1)S(1)} %get-tuple-element.206, bf16[8192,256]{1,0:T(8,128)(2,1)} %get-tuple-element.239, bf16[4096,8192]{1,0:T(8,128)(2,1)} %get-tuple-element.237, s32[]{:T(128)S(6)} %select_n.10, bf16[4096,768]{0,1:T(8,128)(2,1)} %get-tuple-element.238), kind=kOutput, calls=%fused_computation.10.clone.1 | convolution fusion | flops 4307550208 | bytes 21496832 | tf_op jit(solution)/shard_map/while/body/eval_jaxpr/pq,pi->qi/dot_general | solution.py:58
  568.5 9.7 %fusion.65 = f32[8192,256]{0,1:T(8,128)} fusion(bf16[512,256]{0,1:T(8,128)(2,1)S(1)} %get-tuple-element.205, bf16[8192,256]{1,0:T(8,128)(2,1)} %get-tuple-element.239, bf16[4096,8192]{1,0:T(8,128)(2,1)} %get-tuple-element.237, s32[]{:T(128)S(6)} %select_n.10, bf16[4096,768]{0,1:T(8,128)(2,1)} %get-tuple-element.238), kind=kOutput, calls=%fused_computation.9.clone.1 | convolution fusion | flops 4307550208 | bytes 21496832 | tf_op jit(solution)/shard_map/while/body/eval_jaxpr/pq,pi->qi/dot_general | solution.py:58
  578.2 17.0 %maximum_add_fusion.4 = f32[8192,512]{0,1:T(8,128)} fusion(f32[8192,256]{0,1:T(8,128)} %fusion.65, f32[8192,256]{0,1:T(8,128)} %fusion.66, f32[8192,512]{0,1:T(8,128)} %get-tuple-element.223, pred[]{:T(512)S(6)} %compare.3), kind=kLoop, calls=%fused_computation.4.clone.1 | loop fusion | flops 12582912 | bytes 50331648 | tf_op jit(solution)/shard_map/while/body/eval_jaxpr/add | solution.py:66
  595.2 1.2 constant_dynamic-slice_fusion.8
  597.0 4.6 convolution_bitcast_fusion.5
  601.6 4.6 convolution_bitcast_fusion.4
  606.3 9.7 %fusion.66 = f32[8192,256]{0,1:T(8,128)} fusion(bf16[512,256]{0,1:T(8,128)(2,1)S(1)} %get-tuple-element.206, bf16[8192,256]{1,0:T(8,128)(2,1)} %get-tuple-element.239, bf16[4096,8192]{1,0:T(8,128)(2,1)} %get-tuple-element.237, s32[]{:T(128)S(6)} %select_n.10, bf16[4096,768]{0,1:T(8,128)(2,1)} %get-tuple-element.238), kind=kOutput, calls=%fused_computation.10.clone.1 | convolution fusion | flops 4307550208 | bytes 21496832 | tf_op jit(solution)/shard_map/while/body/eval_jaxpr/pq,pi->qi/dot_general | solution.py:58
  615.9 9.7 %fusion.65 = f32[8192,256]{0,1:T(8,128)} fusion(bf16[512,256]{0,1:T(8,128)(2,1)S(1)} %get-tuple-element.205, bf16[8192,256]{1,0:T(8,128)(2,1)} %get-tuple-element.239, bf16[4096,8192]{1,0:T(8,128)(2,1)} %get-tuple-element.237, s32[]{:T(128)S(6)} %select_n.10, bf16[4096,768]{0,1:T(8,128)(2,1)} %get-tuple-element.238), kind=kOutput, calls=%fused_computation.9.clone.1 | convolution fusion | flops 4307550208 | bytes 21496832 | tf_op jit(solution)/shard_map/while/body/eval_jaxpr/pq,pi->qi/dot_general | solution.py:58
  625.6 17.0 %maximum_add_fusion.4 = f32[8192,512]{0,1:T(8,128)} fusion(f32[8192,256]{0,1:T(8,128)} %fusion.65, f32[8192,256]{0,1:T(8,128)} %fusion.66, f32[8192,512]{0,1:T(8,128)} %get-tuple-element.223, pred[]{:T(512)S(6)} %compare.3), kind=kLoop, calls=%fused_computation.4.clone.1 | loop fusion | flops 12582912 | bytes 50331648 | tf_op jit(solution)/shard_map/while/body/eval_jaxpr/add | solution.py:66
  642.6 8.9 %convert_element_type.92 = bf16[8192,512]{0,1:T(8,128)(2,1)} convert(f32[8192,512]{0,1:T(8,128)} %get-tuple-element.116) | non-fusion elementwise | flops 4194304 | bytes 25165824 | tf_op jit(solution)/shard_map/convert_element_type | solution.py:70
  651.6 25.7 %psum.14 = bf16[8192,2]{0,1:T(2,128)(2,1)S(1)} all-reduce(bf16[8192,2]{0,1:T(2,128)(2,1)S(1)} %convert_element_type.89), channel_id=1, replica_groups=mesh['row'=8,'col'=4] {'row'}, use_global_device_ids=true, to_apply=%region_5.0 | all-reduce | flops 16384 | bytes 65536 | tf_op jit(solution)/shard_map/psum | solution.py:71
  677.4 99.4 %all-reduce.2.cloned.1.call-done = bf16[8192,512]{0,1:T(8,128)(2,1)} async-done(((bf16[8192,512]{0,1:T(8,128)(2,1)}), bf16[8192,512]{0,1:T(8,128)(2,1)}) %all-reduce.2.cloned.1.call-update) | async-done | bytes 8388624 | tf_op jit(solution)/shard_map/psum | solution.py:70
  776.8 11.5 %convert_element_type.93 = f32[8192,512]{0,1:T(8,128)} convert(bf16[8192,512]{0,1:T(8,128)(2,1)} %all-reduce.2.cloned.1.call-done) | non-fusion elementwise | flops 4194304 | bytes 25165824 | tf_op jit(solution)/shard_map/convert_element_type | solution.py:70
  788.3 6.2 fusion.29
  794.5 3.1 copy-done
  797.6 3.7 fusion.32
  802.0 20.0 %reduce-scatter.5.cloned.1.call-done = bf16[64,2,256]{2,0,1:T(8,128)(2,1)} async-done(((bf16[256,2,256]{2,0,1:T(8,128)(2,1)}), bf16[64,2,256]{2,0,1:T(8,128)(2,1)}) %reduce-scatter.5.cloned.1.call-update) | async-done | bytes 65552 | tf_op jit(solution)/shard_map/reduce_scatter | solution.py:81
  (76 shorter events, 9.3 us)
Async XLA Ops:
  6.5 104.9 %reduce-scatter.3.cloned.1.call-start = ((), (), s32[]{:S(2)}) async-start(), calls=%async_computation.2 | async-start | bytes 14155776 | tf_op jit(solution)/shard_map/reduce_scatter | solution.py:30
  16.2 134.0 %all-gather.5.cloned.1.call-start = ((), (), s32[]{:S(2)}) async-start(), calls=%async_computation.4 | async-start | bytes 4718592 | tf_op jit(solution)/shard_map/all_gather | solution.py:33
  113.3 153.8 %all-gather.3.cloned.1.call-start = ((), (), s32[]{:S(2)}) async-start(), calls=%async_computation.3 | async-start | bytes 7864320 | tf_op jit(solution)/shard_map/all_gather | solution.py:40
  114.1 662.7 %all-reduce.2.cloned.1.call-start = ((), (), s32[]{:S(2)}) async-start(), calls=%async_computation.5 | async-start | bytes 16777216 | tf_op jit(solution)/shard_map/psum | solution.py:70
  651.5 170.5 %reduce-scatter.5.cloned.1.call-start = ((), (), s32[]{:S(2)}) async-start(), calls=%async_computation.6 | async-start | bytes 327680 | tf_op jit(solution)/shard_map/reduce_scatter | solution.py:81
  776.8 11.5 %copy-start.1 = (bf16[8192,256]{0,1:T(8,128)(2,1)S(1)}, bf16[8192,256]{0,1:T(8,128)(2,1)}, u32[]{:S(2)}) copy-start(bf16[8192,256]{0,1:T(8,128)(2,1)} %all-gather.5.cloned.1.call-done) | copy-start | bytes 12582916
  788.3 9.3 %copy-start = (f32[8192,512]{0,1:T(8,128)S(1)}, f32[8192,512]{0,1:T(8,128)}, u32[]{:S(2)}) copy-start(f32[8192,512]{0,1:T(8,128)} %convert_element_type.93) | copy-start | bytes 50331652
Sparse Core Ops, SparseCore 0:
  16.3 95.0 reduce-scatter.2
  113.5 36.6 all-gather.4
  151.8 115.3 all-gather.2
  651.7 125.0 all-reduce.1
  802.1 19.8 reduce-scatter.4
where the time goes:
time: 831 us; the launch traced here: 830 us
  waiting for transfers between devices  362 us (44%)
  matrix products  246 us (30%)
  other arithmetic  158 us (19%)
  blocking collectives  25.7 us (3%)
  local copies, waits for them, and re-layouts  24.6 us (3%)
  between operations  13.2 us (2%)
    dot_general x16, matrix products, advance(): jnp.einsum('pq,pi->qi', amplitude, x_rows, preferred_element_type=jnp.flo...  155 us
    add x8, other arithmetic, advance(): k_total + jnp.concatenate(k_parts, axis=1)  132 us
    all_gather x1, waiting for transfers between devices, on_device(): shard_rows = lax.all_gather(own_points, 'col', axis=0, tiled=True)  111 us
    psum x1, waiting for transfers between devices, on_device(): lax.psum(k_total.astype(jnp.bfloat16), 'row').astype(jnp.float32)  99.4 us
    reduce_scatter x1, waiting for transfers between devices, on_device(): lax.psum_scatter(partial_value.astype(jnp.bfloat16), 'row', scatter_dimen...  95.2 us
    dot_general x16, matrix products, advance(): jnp.einsum('p,pq->q', density, v_rows, preferred_element_type=jnp.float32)  73.3 us
    all_gather x1, waiting for transfers between devices, on_device(): lax.all_gather(own_points[:, :occupied], 'row', axis=0, tiled=True)  36.1 us
    psum x1, blocking collectives, on_device(): lax.psum(u_total.astype(jnp.bfloat16), 'row').astype(jnp.float32)  25.7 us
  transfers between devices with their start and end apart: 5, of which 5 were waited for; matrix products, arithmetic and copies ran while one was open for 1% of the time, Pallas kernels for 0%

commit v1 on v0

v1 whole, which is shorter than its diff:
```python
import functools
import math

import jax
import jax.numpy as jnp
from jax import lax
from jax.experimental import pallas as pl
from jax.experimental.pallas import tpu as pltpu
from jax.sharding import PartitionSpec as P

P_SIZE = 32768
NT = (((1,), (1,)), ((), ()))


def force_kernel(walkers, occupied, sub, th_ref, xt_ref, d_ref, xq_ref, xqt_ref, v_ref, o_ref, acc, uacc):
    step, steps = pl.program_id(1), pl.num_programs(1)

    @pl.when(step == 0)
    def _():
        acc[...] = jnp.zeros_like(acc)
        uacc[...] = jnp.zeros_like(uacc)

    for j in range(v_ref.shape[2] // sub):
        qs = slice(j * sub, (j + 1) * sub)
        v = v_ref[0, :, qs]
        for w in range(walkers):
            rows = slice(w * occupied, (w + 1) * occupied)
            tile = lax.dot_general(th_ref[w], xq_ref[qs, :], NT, preferred_element_type=jnp.float32)
            amplitude = tile.astype(jnp.bfloat16) * v
            acc[rows, qs] += jnp.dot(xt_ref[...], amplitude, preferred_element_type=jnp.float32)
        uacc[:, qs] += jnp.dot(d_ref[...], v, preferred_element_type=jnp.float32)

    @pl.when(step == steps - 1)
    def _():
        for w in range(walkers):
            rows = slice(w * occupied, (w + 1) * occupied)
            o_ref[rows, :] = (
                uacc[w : w + 1] * xqt_ref[...].astype(jnp.float32) - acc[rows, :]
            ).astype(jnp.bfloat16)


def partial_forces(theta, x_rows_t, density, x_cols, x_cols_t, coulomb):
    a, b, q = coulomb.shape
    walkers, _, n = theta.shape
    tp, tq = math.gcd(b, 1024), math.gcd(q, 1024)
    sub = math.gcd(tq, 512)
    bp = b // tp
    return pl.pallas_call(
        functools.partial(force_kernel, walkers, n, sub),
        grid=(q // tq, a * bp),
        in_specs=[
            pl.BlockSpec((walkers, tp, n), lambda j, p: (0, p, 0)),
            pl.BlockSpec((n, tp), lambda j, p: (0, p)),
            pl.BlockSpec((density.shape[0], tp), lambda j, p: (0, p)),
            pl.BlockSpec((tq, n), lambda j, p: (j, 0)),
            pl.BlockSpec((n, tq), lambda j, p: (0, j)),
            pl.BlockSpec((1, tp, tq), lambda j, p: (p // bp, p % bp, j)),
        ],
        out_specs=pl.BlockSpec((walkers * n, tq), lambda j, p: (0, j)),
        out_shape=jax.ShapeDtypeStruct((walkers * n, q), jnp.bfloat16),
        scratch_shapes=[
            pltpu.VMEM((walkers * n, tq), jnp.float32),
            pltpu.VMEM((density.shape[0], tq), jnp.float32),
        ],
        compiler_params=pltpu.CompilerParams(vmem_limit_bytes=48 << 20),
    )(theta, x_rows_t, density, x_cols, x_cols_t, coulomb)


def on_device(collocation, greens, trial_orbitals, coulomb):
    walkers, occupied, basis_local = greens.shape
    stacked = jnp.concatenate([trial_orbitals[None], greens], axis=0).reshape(
        (walkers + 1) * occupied, basis_local
    )
    own_collocation = lax.all_to_all(collocation, "row", split_axis=0, concat_axis=1, tiled=True)
    all_stacked = lax.all_gather(stacked, "row", axis=1, tiled=True)
    own_points = lax.dot_general(
        own_collocation, all_stacked, NT, preferred_element_type=jnp.float32
    ).astype(jnp.bfloat16)
    x_cols = lax.all_gather(own_points[:, :occupied], "row", axis=0, tiled=True)
    shard_rows = lax.all_gather(own_points, "col", axis=0, tiled=True)
    x_rows = shard_rows[:, :occupied]
    theta = jnp.stack(
        [shard_rows[:, (w + 1) * occupied : (w + 2) * occupied] for w in range(walkers)]
    )
    density = jnp.sum(
        x_rows.astype(jnp.float32)[None] * theta.astype(jnp.float32), axis=2
    ).astype(jnp.bfloat16)
    density = jnp.pad(density, ((0, -walkers % 16), (0, 0)))
    forces = partial_forces(theta, x_rows.T, density, x_cols, x_cols.T, coulomb)
    forces = lax.psum(forces, "row")
    terms = jnp.dot(forces, collocation, preferred_element_type=jnp.float32)
    terms = terms.astype(jnp.bfloat16).reshape(walkers, occupied, basis_local).transpose(1, 0, 2)
    gradient = lax.psum_scatter(terms, "col", scatter_dimension=0, tiled=True).astype(jnp.float32)
    return (gradient * P_SIZE ** (-0.5)).astype(jnp.bfloat16)


def solution(mesh):
    return jax.shard_map(
        on_device,
        mesh=mesh,
        in_specs=(P("col", "row"), P(None, None, "row"), P(None, "row"), P(None, "row", "col")),
        out_specs=P("col", None, "row"),
        check_vma=False,
    )
```

time: 831 us -> 529 us (0.64)
  matrix products: 246 us -> 13.4 us
  other arithmetic: 158 us -> 10.5 us
  Pallas kernels: 0 us -> 95.5 us
  waiting for transfers between devices: 362 us -> 306 us
  blocking collectives: 25.7 us -> 67 us
    dot_general x35 -> x2, matrix products: 246 us -> 13.4 us  [the longest x1 6.9 us: on_device(): terms = jnp.dot(forces, collocation, preferred_element_type=jnp.float32)]
    add x16 -> x0, other arithmetic: 133 us -> none  [the longest x8 132 us: advance(): k_total + jnp.concatenate(k_parts, axis=1)]
    reduce_scatter x2 -> x0, waiting for transfers between devices: 115 us -> none  [the longest x1 95.2 us: on_device(): lax.psum_scatter(partial_value.astype(jnp.bfloat16), 'row', scatter_dimen...]
    pallas_call x0 -> x1, Pallas kernels: none -> 95.5 us  [partial_forces(): pl.pallas_call(functools.partial(force_kernel, walkers, n, sub), grid=(q...]
    all_to_all x0 -> x1, blocking collectives: none -> 67 us  [on_device(): lax.all_to_all(collocation, 'row', split_axis=0, concat_axis=1, tiled=True)]
    unnamed x5 -> x6, waiting for transfers between devices: 0.75 us -> 34.9 us
    psum x1 -> x0, blocking collectives: 25.7 us -> none  [on_device(): lax.psum(u_total.astype(jnp.bfloat16), 'row').astype(jnp.float32)]
    psum x1, waiting for transfers between devices: 99.4 us -> 125 us  [on_device(): forces = lax.psum(forces, 'row')]
  transfers between devices with their start and end apart: 5 -> 5, of which waited for: 5 -> 4; matrix products, arithmetic and copies ran while one was open for 1% -> 3% of each run, Pallas kernels for 0% -> 0%
where the time goes in v1:
time: 529 us
  waiting for transfers between devices  306 us (58%)
  Pallas kernels  95.5 us (18%)
  blocking collectives  67 us (13%)
  local copies, waits for them, and re-layouts  22 us (4%)
  between operations  13.9 us (3%)
  matrix products  13.4 us (3%)
  other arithmetic  10.5 us (2%)
    psum x1, waiting for transfers between devices, on_device(): forces = lax.psum(forces, 'row')  125 us
    all_gather x1, waiting for transfers between devices, on_device(): shard_rows = lax.all_gather(own_points, 'col', axis=0, tiled=True)  111 us
    pallas_call x1, Pallas kernels, partial_forces(): pl.pallas_call(functools.partial(force_kernel, walkers, n, sub), grid=(q...  95.5 us
    all_to_all x1, blocking collectives, on_device(): lax.all_to_all(collocation, 'row', split_axis=0, concat_axis=1, tiled=True)  67 us
    all_gather x1, waiting for transfers between devices, on_device(): x_cols = lax.all_gather(own_points[:, :occupied], 'row', axis=0, tiled=True)  36.1 us
    unnamed x6, waiting for transfers between devices  34.9 us
  transfers between devices with their start and end apart: 5, of which 4 were waited for; matrix products, arithmetic and copies ran while one was open for 3% of the time, Pallas kernels for 0%

profile of v1, /device:TPU:0, one launch (start us, length us, event | category | flops | bytes accessed | tf_op | source)
XLA Modules:
  0.0 528.8 jit_solution(17550928558327738881)
XLA Ops:
  6.5 0.0 all-gather.4.cloned.1.call-start
  6.5 1.8 pad_maximum_fusion.1
  8.3 0.0 all-gather.4.cloned.1.call-update
  8.3 0.0 all-gather.8.cloned.1.call-start
  8.4 67.0 %all_to_all.19 = bf16[8,1024,256]{2,1,0:T(8,128)(2,1)} all-to-all(bf16[8,1024,256]{2,1,0:T(8,128)(2,1)} %bitcast.25), channel_id=1, replica_groups=mesh['row'=8,'col'=4] {'row'}, dimensions={0} | all-to-all | bytes 8388608 | tf_op jit(solution)/shard_map/all_to_all | solution.py:74
  75.4 6.4 %copy.15 = bf16[1024,8,256]{0,2,1:T(8,128)(2,1)} copy(bf16[1024,8,256]{2,0,1:T(8,128)(2,1)} %bitcast.24) | data formatting | bytes 8388608 | tf_op jit(solution)/shard_map/all_to_all | solution.py:74
  81.8 0.0 all-gather.4.cloned.1.call-done
  81.8 6.6 %fusion = bf16[1024,768]{0,1:T(8,128)(2,1)S(1)} fusion(bf16[768,2048]{1,0:T(8,128)(2,1)} %all-gather.4.cloned.1.call-done, bf16[1024,2048]{0,1:T(8,128)(2,1)} %bitcast.26), kind=kOutput, calls=%fused_computation.7 | convolution fusion | flops 3222011904 | bytes 8912896 | tf_op jit(solution)/shard_map/dot_general | solution.py:76
  88.4 0.0 copy-start
  88.4 0.9 slice.19
  89.3 0.0 all-gather.8.cloned.1.call-update
  89.3 0.0 all-gather.6.cloned.1.call-start
  89.4 0.3 copy-done
  89.7 0.4 all-gather.6.cloned.1.call-update
  90.1 0.0 all-reduce.5.cloned.1.call-start
  90.1 36.1 %all-gather.8.cloned.1.call-done = bf16[8192,256]{0,1:T(8,128)(2,1)} async-done(((bf16[1024,256]{0,1:T(8,128)(2,1)}), bf16[8192,256]{0,1:T(8,128)(2,1)}) %all-gather.8.cloned.1.call-update) | async-done | bytes 4194320 | tf_op jit(solution)/shard_map/all_gather | solution.py:79
  126.2 6.4 %copy.17.xq_ref = bf16[8192,256]{1,0:T(8,128)(2,1)} copy(bf16[8192,256]{0,1:T(8,128)(2,1)} %all-gather.8.cloned.1.call-done) | data formatting | bytes 8388608 | tf_op jit(solution)/shard_map/all_gather | solution.py:79
  132.6 110.6 %all-gather.6.cloned.1.call-done = bf16[4096,768]{0,1:T(8,128)(2,1)} async-done(((bf16[1024,768]{0,1:T(8,128)(2,1)}), bf16[4096,768]{0,1:T(8,128)(2,1)}) %all-gather.6.cloned.1.call-update) | async-done | bytes 6291472 | tf_op jit(solution)/shard_map/all_gather | solution.py:80
  243.2 3.8 slice_convert_fusion
  247.0 2.3 pad_maximum_fusion
  249.3 1.0 multiply_reduce_fusion
  250.4 6.3 %copy.16.th_ref = bf16[2,4096,256]{2,1,0:T(8,128)(2,1)} copy(bf16[2,4096,256]{1,2,0:T(8,128)(2,1)} %pad_maximum_fusion) | data formatting | bytes 8388608 | tf_op jit(solution)/shard_map/stack | solution.py:82
  256.7 95.5 %shard_map.46 = bf16[512,8192]{1,0:T(8,128)(2,1)} custom-call(bf16[2,4096,256]{2,1,0:T(8,128)(2,1)} %copy.16.th_ref, bf16[256,4096]{1,0:T(8,128)(2,1)S(1)} %get-tuple-element.6.xt_ref, bf16[16,4096]{1,0:T(8,128)(2,1)S(1)} %pad.4.d_ref, bf16[8192,256]{1,0:T(8,128)(2,1)} %copy.17.xq_ref, bf16[256,8192]{1,0:T(8,128)(2,1)} %bitcast.23, bf16[4,1024,8192]{2,1,0:T(8,128)(2,1)} %v_ref.1), custom_call_target="tpu_custom_call" | custom-call | tf_op jit(solution)/shard_map/pallas_call | solution.py:48
  352.2 0.0 all-reduce.5.cloned.1.call-update
  352.2 0.0 copy-start.1
  352.2 0.0 all-reduce.7.cloned.1.call-start
  352.3 124.9 %all-reduce.5.cloned.1.call-done = bf16[512,8192]{1,0:T(8,128)(2,1)} async-done(((bf16[512,8192]{1,0:T(8,128)(2,1)}), bf16[512,8192]{1,0:T(8,128)(2,1)}) %all-reduce.5.cloned.1.call-update) | async-done | bytes 8388624 | tf_op jit(solution)/shard_map/psum | solution.py:90
  477.1 6.9 %convolution_convert_fusion.1 = bf16[512,256]{1,0:T(8,128)(2,1)S(1)} fusion(bf16[512,8192]{1,0:T(8,128)(2,1)} %all-reduce.5.cloned.1.call-done, bf16[8192,256]{1,0:T(8,128)(2,1)} %param.4), kind=kOutput, calls=%fused_computation.8 | convolution fusion | flops 2147614720 | bytes 12845056 | tf_op jit(solution)/shard_map/dot_general | solution.py:91
  484.0 1.0 copy.20
  485.0 0.0 all-reduce.7.cloned.1.call-update
  485.0 0.0 copy-done.1
  485.1 0.6 dynamic-slice
  486.3 34.5 %all-reduce.7.cloned.1.call-done = bf16[256,2,256]{2,1,0:T(2,128)(2,1)} async-done(((bf16[256,2,256]{2,1,0:T(2,128)(2,1)}), bf16[256,2,256]{2,1,0:T(2,128)(2,1)}) %all-reduce.7.cloned.1.call-update) | async-done | bytes 262160
  520.7 1.5 multiply_convert_fusion
  (1 shorter events, 0.0 us)
Async XLA Ops:
  6.5 75.3 %all-gather.4.cloned.1.call-start = ((), (), s32[]{:S(2)}) async-start(), calls=%async_computation.1 | async-start | bytes 3538944 | tf_op jit(solution)/shard_map/all_gather | solution.py:75
  8.3 117.9 %all-gather.8.cloned.1.call-start = ((), (), s32[]{:S(2)}) async-start(), calls=%async_computation.3 | async-start | bytes 4718592 | tf_op jit(solution)/shard_map/all_gather | solution.py:79
  88.4 1.4 copy-start
  89.3 153.9 %all-gather.6.cloned.1.call-start = ((), (), s32[]{:S(2)}) async-start(), calls=%async_computation.2 | async-start | bytes 7864320 | tf_op jit(solution)/shard_map/all_gather | solution.py:80
  90.1 387.1 %all-reduce.5.cloned.1.call-start = ((), (), s32[]{:S(2)}) async-start(), calls=%async_computation.4 | async-start | bytes 16777216 | tf_op jit(solution)/shard_map/psum | solution.py:90
  352.2 132.8 %copy-start.1 = (u32[32]{0:T(128)S(1)}, u32[32]{0:T(128)}, u32[]{:S(2)}) copy-start(u32[32]{0:T(128)} %constant.11) | copy-start | bytes 388
  352.2 168.5 %all-reduce.7.cloned.1.call-start = ((), (), s32[]{:S(2)}) async-start(), calls=%async_computation.5 | async-start | bytes 524288
Sparse Core Ops, SparseCore 0:
  9.2 61.1 all-gather.3
  89.5 36.7 all-gather.7
  127.8 115.3 all-gather.5
  352.3 124.7 all-reduce.4
  485.2 35.5 all-reduce.6
